TPU v7x, 32 devices: a whole 2x2x4 slice. The times are simulated.
32 devices in a mesh: row: 4 (over z), col: 8 (over y, x, core).
Axes of the slice: x: 2, y: 2, z: 4, core: 2. Of those that a mesh axis runs over, the one named last changes fastest.
Arguments:
- activations: bfloat16 [96, 48, 3072], P('row', None, 'col'), may hold values from -30 to 30
- cotangent: bfloat16 [96, 48, 3072], P('row', None, 'col'), may hold values from -6 to 6
- kernel: float32 [7, 7, 3072], P(None, None, 'col'), may hold values from -0.875 to 0.875
- ln_gain: float32 [3072], replicated, may hold values from 0.25 to 1.75
- ln_bias: float32 [3072], replicated, may hold values from -3 to 3
- w_expand: bfloat16 [3072, 12288], P('row', 'col'), may hold values from -0.5 to 0.5
- b_expand: float32 [12288], P('col'), may hold values from -3 to 3
- w_reduce: bfloat16 [12288, 3072], P('col', 'row'), may hold values from -0.078125 to 0.078125
- b_reduce: float32 [3072], P('col'), may hold values from -3 to 3
- layer_scale: float32 [3072], P('col'), may hold values from 0.3 to 1.5
Outputs:
- block_out: bfloat16 [96, 48, 3072], P('row', None, 'col')
- grad_input: bfloat16 [96, 48, 3072], P('row', None, 'col')
All inputs are finite; a program needn't handle non-finite values.
Results may differ from a plain program's by a relative error of at most 0.015.
Values may be sent and summed in bfloat16 or wider, within the bound.
A program may use at most 128 MiB of HBM per device.

v0:
```python
import jax
import jax.numpy as jnp
from jax import lax
from jax.sharding import PartitionSpec as P

H = 48
epsilon = 1e-06
root_half = 0.7071067811865476
density_scale = 0.3989422804014327


def spatial_mix(padded, weights, height):
    row_count = padded.shape[0] - 6
    col_count = padded.shape[1] - 6
    out_rows = jnp.arange(row_count, dtype=jnp.int32)
    running = jnp.zeros((row_count, col_count, padded.shape[2]), jnp.float32)
    for row_off in range(7):
        source = out_rows + (row_off - 3)
        inside = source // height == out_rows // height
        band = jnp.zeros_like(running)
        for col_off in range(7):
            band = (
                band
                + weights[row_off, col_off]
                * padded[row_off : row_off + row_count, col_off : col_off + col_count]
            )
        running = running + jnp.where(inside[:, None, None], band, jnp.zeros_like(band))
    return running


def gelu_slope(preact):
    cumulative = 0.5 * (1.0 + jax.scipy.special.erf(preact * root_half))
    return cumulative + preact * jnp.exp(-0.5 * preact * preact) * density_scale


def channel_sums(first_sum, second_sum):
    return lax.psum((first_sum, second_sum), "col")


def body(
    activations,
    cotangent,
    kernel,
    ln_gain,
    ln_bias,
    w_expand,
    b_expand,
    w_reduce,
    b_reduce,
    layer_scale,
):
    row_count, grid_width, narrow = activations.shape
    channels = narrow * lax.axis_size("col")
    col_start = lax.axis_index("col") * narrow
    tokens = row_count * grid_width
    flipped = kernel[::-1, ::-1]

    def mixing(source_field, weights):
        gathered = lax.all_to_all(source_field, "row", split_axis=2, concat_axis=0, tiled=True)
        per_device = gathered.shape[2]
        subset = lax.dynamic_slice_in_dim(
            weights, lax.axis_index("row") * per_device, per_device, 2
        )
        padded = jnp.pad(gathered, ((3, 3), (3, 3), (0, 0))).astype(jnp.float32)
        mixed_out = spatial_mix(padded, subset, H).astype(jnp.bfloat16)
        return lax.all_to_all(mixed_out, "row", split_axis=0, concat_axis=2, tiled=True)

    mixed_bf = mixing(activations, kernel)
    mixed_flat = lax.optimization_barrier(mixed_bf).reshape(tokens, narrow)
    expand_full, reduce_full = (
        lax.all_gather(w_expand, "row", axis=0, tiled=True),
        lax.all_gather(w_reduce, "row", axis=1, tiled=True),
    )
    local_mixed = mixed_flat.astype(jnp.float32)
    row_sum, square_sum = channel_sums(
        jnp.sum(local_mixed, 1), jnp.sum(local_mixed * local_mixed, 1)
    )
    row_mean = row_sum[:, None] / channels
    square = square_sum[:, None] / channels
    inv_std = lax.rsqrt(square - row_mean * row_mean + epsilon)
    normal_local = (local_mixed - row_mean) * inv_std
    local_gain = lax.dynamic_slice_in_dim(ln_gain, col_start, narrow)
    local_shift = lax.dynamic_slice_in_dim(ln_bias, col_start, narrow)
    normed = (normal_local * local_gain + local_shift).astype(jnp.bfloat16)
    panel = expand_full
    preact = jnp.dot(
        lax.all_gather(normed, "col", axis=1, tiled=True), panel, preferred_element_type=jnp.float32
    )
    preact = preact + b_expand
    hidden = jax.nn.gelu(preact, approximate=False).astype(jnp.bfloat16)
    panel = reduce_full
    branch_turned = lax.psum_scatter(
        lax.dot_general(
            panel, hidden, (((0,), (1,)), ((), ())), preferred_element_type=jnp.float32
        ).astype(jnp.bfloat16),
        "col",
        scatter_dimension=0,
        tiled=True,
    ).astype(jnp.float32)
    branch_out = branch_turned.T + b_reduce
    act_f = activations.astype(jnp.float32)
    block_out = (act_f + layer_scale * branch_out.reshape(row_count, grid_width, narrow)).astype(
        jnp.bfloat16
    )
    cot_f = cotangent.astype(jnp.float32)
    grad_branch = (layer_scale * cot_f).reshape(tokens, narrow).astype(jnp.bfloat16)
    panel = reduce_full
    grad_hidden = lax.dot_general(
        lax.all_gather(grad_branch, "col", axis=1, tiled=True),
        panel,
        (((1,), (1,)), ((), ())),
        preferred_element_type=jnp.float32,
    )
    grad_preact = (grad_hidden * gelu_slope(preact)).astype(jnp.bfloat16)
    panel = expand_full
    grad_turned = lax.psum_scatter(
        lax.dot_general(
            panel, grad_preact, (((1,), (1,)), ((), ())), preferred_element_type=jnp.float32
        ).astype(jnp.bfloat16),
        "col",
        scatter_dimension=0,
        tiled=True,
    ).astype(jnp.float32)
    grad_gain = grad_turned.T * local_gain
    grad_total, grad_cross = channel_sums(
        jnp.sum(grad_gain, 1), jnp.sum(grad_gain * normal_local, 1)
    )
    grad_mixed = inv_std * (
        grad_gain - grad_total[:, None] / channels - normal_local * grad_cross[:, None] / channels
    )
    grad_mixed = grad_mixed.astype(jnp.bfloat16).reshape(row_count, grid_width, narrow)
    grad_spatial = mixing(grad_mixed, flipped)
    grad_input = (cot_f + lax.optimization_barrier(grad_spatial).astype(jnp.float32)).astype(
        jnp.bfloat16
    )
    return (block_out, grad_input)


def solution(mesh):
    return jax.shard_map(
        body,
        mesh=mesh,
        in_specs=(
            P("row", None, "col"),
            P("row", None, "col"),
            P(None, None, "col"),
            P(),
            P(),
            P("row", "col"),
            P("col"),
            P("col", "row"),
            P("col"),
            P("col"),
        ),
        out_specs=(P("row", None, "col"), P("row", None, "col")),
        check_vma=False,
    )
```

profile of v0, /device:TPU:2, one launch (start us, length us, event | category | flops | bytes accessed | tf_op | source)
XLA Modules:
  0.0 833.0 jit_solution(8400221531538594373)
XLA Ops:
  7.2 0.7 all-gather.7.cloned.1.call-update
  8.3 1.4 copy.16
  9.8 4.6 reshape.134
  14.4 4.9 all-to-all-start
  21.0 2.2 fusion.181
  23.2 46.9 %all-to-all-done = bf16[4,2,55296]{2,1,0:T(2,128)(2,1)S(1)} async-done(((bf16[4,2,55296]{2,1,0:T(2,128)(2,1)}), bf16[4,2,55296]{2,1,0:T(2,128)(2,1)S(1)}, u32[]{:S(2)}, u32[]{:S(2)}) %all-to-all-start) | async-done | bytes 884768 | tf_op jit(solution)/shard_map/all_to_all | solution.py:59
  70.1 2.4 reshape.135
  72.5 2.1 copy.24
  76.0 20.2 %fusion.115 = bf16[96,48,96]{2,1,0:T(8,128)(2,1)} fusion(f32[102,54,96]{2,1,0:T(8,128)S(1)} %pad_convert_fusion.1, f32[96]{0:T(128)} %get-tuple-element.105, f32[96]{0:T(128)S(1)} %get-tuple-element.58, f32[96]{0:T(128)S(1)} %get-tuple-element.59, f32[96]{0:T(128)S(1)} %get-tuple-element.60, f32[96]{0:T(128)S(1)} %copy-done.55, f32[96]{0:T(128)S(1)} %copy-done.56, ...), kind=kLoop, calls=%fused_computation.178 | loop fusion | flops 46006272 | bytes 87608256 | tf_op jit(solution)/shard_map/convert_element_type | solution.py:65
  96.2 3.5 all-to-all-start.1
  99.8 0.8 dynamic_slice.13
  100.5 0.8 dynamic_slice.14
  101.3 54.6 %all-to-all-done.1 = bf16[96,48,96]{2,1,0:T(8,128)(2,1)S(1)} async-done(((bf16[96,48,96]{2,1,0:T(8,128)(2,1)}), bf16[96,48,96]{2,1,0:T(8,128)(2,1)S(1)}, u32[]{:S(2)}, u32[]{:S(2)}) %all-to-all-start.1) | async-done | bytes 884768 | tf_op jit(solution)/shard_map/all_to_all | solution.py:66
  155.9 0.9 copy.19
  156.8 0.8 all_to_all.59
  158.1 21.4 %all-reduce.3 = (f32[1152]{0:T(1024)S(1)}, f32[1152]{0:T(1024)S(1)}) all-reduce(f32[1152]{0:T(1024)S(1)} %reduce_sum.43, f32[1152]{0:T(1024)S(1)} %reduce_sum.41), channel_id=1, replica_groups=mesh['row'=4,'col'=8] {'col'}, use_global_device_ids=true, to_apply=%region_3.4 | all-reduce | flops 2304 | bytes 18432 | tf_op jit(solution)/shard_map/psum | solution.py:37
  180.2 1.3 add_convert_fusion.1
  181.6 0.7 all-gather.9.cloned.1.call-update
  182.8 36.2 %all-gather.7.cloned.1.call-done = bf16[3072,1536]{1,0:T(8,128)(2,1)} async-done(((bf16[768,1536]{1,0:T(8,128)(2,1)}), bf16[3072,1536]{1,0:T(8,128)(2,1)}) %all-gather.7.cloned.1.call-update) | async-done | bytes 9437200 | tf_op jit(solution)/shard_map/all_gather | solution.py:71
  219.0 51.8 %all-gather.5.cloned.1.call-done = bf16[1152,3072]{1,0:T(8,128)(2,1)} async-done(((bf16[1152,384]{1,0:T(8,128)(2,1)}), bf16[1152,3072]{1,0:T(8,128)(2,1)}) %all-gather.5.cloned.1.call-update) | async-done | bytes 7077904 | tf_op jit(solution)/shard_map/all_gather | solution.py:87
  270.8 17.0 %convolution_add_fusion = f32[1152,1536]{1,0:T(8,128)} fusion(bf16[1152,3072]{1,0:T(8,128)(2,1)} %all-gather.5.cloned.1.call-done, bf16[3072,1536]{1,0:T(8,128)(2,1)} %all-gather.7.cloned.1.call-done, f32[1536]{0:T(1024)S(1)} %copy-done.95), kind=kOutput, calls=%fused_computation.7 | convolution fusion | flops 10873405440 | bytes 23599104 | tf_op jit(solution)/shard_map/dot_general | solution.py:86
  287.8 151.4 %all-gather.9.cloned.1.call-done = bf16[1536,3072]{1,0:T(8,128)(2,1)} async-done(((bf16[1536,768]{1,0:T(8,128)(2,1)}), bf16[1536,3072]{1,0:T(8,128)(2,1)}) %all-gather.9.cloned.1.call-update) | async-done | bytes 9437200 | tf_op jit(solution)/shard_map/all_gather | solution.py:72
  439.2 31.1 %fusion = bf16[3072,1152]{0,1:T(8,128)(2,1)} fusion(bf16[1536,3072]{1,0:T(8,128)(2,1)} %all-gather.9.cloned.1.call-done, f32[1152,1536]{1,0:T(8,128)} %convolution_add_fusion), kind=kOutput, calls=%fused_computation.5 | convolution fusion | flops 10990190592 | bytes 23592960 | tf_op jit(solution)/shard_map/dot_general | solution.py:93
  470.2 9.8 %copy.26 = bf16[3072,1152]{1,0:T(8,128)(2,1)} copy(bf16[3072,1152]{0,1:T(8,128)(2,1)} %fusion) | data formatting | bytes 14155776
  480.2 63.7 %reduce-scatter.7.cloned.1.call-done = bf16[384,1152]{1,0:T(8,128)(2,1)} async-done(((bf16[3072,1152]{1,0:T(8,128)(2,1)}), bf16[384,1152]{1,0:T(8,128)(2,1)}) %reduce-scatter.7.cloned.1.call-update) | async-done | bytes 884752
  543.9 1.7 copy.27
  545.8 1.7 fusion.167
  547.7 50.2 %all-gather.11.cloned.1.call-done = bf16[1152,3072]{1,0:T(8,128)(2,1)} async-done(((bf16[1152,384]{1,0:T(8,128)(2,1)}), bf16[1152,3072]{1,0:T(8,128)(2,1)}) %all-gather.11.cloned.1.call-update) | async-done | bytes 7077904 | tf_op jit(solution)/shard_map/all_gather | solution.py:109
  597.9 18.7 %fusion.2.clone.4 = bf16[1152,1536]{1,0:T(8,128)(2,1)S(1)} fusion(bf16[1152,3072]{1,0:T(8,128)(2,1)} %all-gather.11.cloned.1.call-done, bf16[1536,3072]{1,0:T(8,128)(2,1)} %all-gather.9.cloned.1.call-done, f32[1152,1536]{1,0:T(8,128)} %convolution_add_fusion), kind=kOutput, calls=%fused_computation.8.clone.clone.clone.1 | convolution fusion | flops 10889330688 | bytes 27131904 | tf_op jit(solution)/shard_map/dot_general | solution.py:108
  616.5 15.6 %fusion.1 = bf16[3072,1152]{0,1:T(8,128)(2,1)} fusion(bf16[3072,1536]{1,0:T(8,128)(2,1)} %all-gather.7.cloned.1.call-done, bf16[1152,1536]{1,0:T(8,128)(2,1)S(1)} %fusion.2.clone.4), kind=kOutput, calls=%fused_computation.6 | convolution fusion | flops 10875174912 | bytes 20054016 | tf_op jit(solution)/shard_map/dot_general | solution.py:117
  632.1 10.3 %copy.28 = bf16[3072,1152]{1,0:T(8,128)(2,1)} copy(bf16[3072,1152]{0,1:T(8,128)(2,1)} %fusion.1) | data formatting | bytes 14155776
  642.5 65.6 %reduce-scatter.9.cloned.1.call-done = bf16[384,1152]{1,0:T(8,128)(2,1)} async-done(((bf16[3072,1152]{1,0:T(8,128)(2,1)}), bf16[384,1152]{1,0:T(8,128)(2,1)}) %reduce-scatter.9.cloned.1.call-update) | async-done | bytes 884752
  708.1 1.7 copy.29
  710.1 0.7 fusion.172
  710.9 21.2 %all-reduce.2 = (f32[1152]{0:T(1024)S(1)}, f32[1152]{0:T(1024)S(1)}) all-reduce(f32[1152]{0:T(1024)S(1)} %fusion.172, f32[1152]{0:T(1024)S(1)} %fusion.174), channel_id=1, replica_groups=mesh['row'=4,'col'=8] {'col'}, use_global_device_ids=true, to_apply=%region_9.10 | all-reduce | flops 2304 | bytes 18432 | tf_op jit(solution)/shard_map/psum | solution.py:37
  732.0 1.0 fusion.171
  733.0 1.4 copy.20
  734.4 4.6 reshape.136
  739.1 4.6 all-to-all-start.2
  743.8 1.0 fusion.180
  744.8 22.0 %all-to-all-done.2 = bf16[4,2,55296]{2,1,0:T(2,128)(2,1)S(1)} async-done(((bf16[4,2,55296]{2,1,0:T(2,128)(2,1)}), bf16[4,2,55296]{2,1,0:T(2,128)(2,1)S(1)}, u32[]{:S(2)}, u32[]{:S(2)}) %all-to-all-start.2) | async-done | bytes 884768 | tf_op jit(solution)/shard_map/all_to_all | solution.py:59
  766.7 2.4 reshape.137
  769.2 2.1 copy.25
  772.6 19.4 %fusion.60 = bf16[96,48,96]{2,1,0:T(8,128)(2,1)S(1)} fusion(f32[102,54,96]{2,1,0:T(8,128)S(1)} %pad_convert_fusion, f32[96]{0:T(128)} %get-tuple-element.56, f32[96]{0:T(128)S(1)} %get-tuple-element.9, f32[96]{0:T(128)S(1)} %get-tuple-element.10, f32[96]{0:T(128)S(1)} %get-tuple-element.11, f32[96]{0:T(128)S(1)} %copy-done.15, f32[96]{0:T(128)S(1)} %copy-done.16, ...), kind=kLoop, calls=%fused_computation.74 | loop fusion | flops 46006272 | bytes 87608256 | tf_op jit(solution)/shard_map/convert_element_type | solution.py:65
  792.1 31.0 %all_to_all.72 = bf16[96,48,96]{2,1,0:T(8,128)(2,1)S(1)} all-to-all(bf16[96,48,96]{2,1,0:T(8,128)(2,1)S(1)} %fusion.60), channel_id=1, replica_groups=mesh['row'=4,'col'=8] {'row'}, dimensions={0} | all-to-all | bytes 1769472 | tf_op jit(solution)/shard_map/all_to_all | solution.py:66
  823.1 0.9 copy.23
  824.0 0.8 all_to_all.67
  824.8 1.1 fusion.168
  (217 shorter events, 6.2 us)
Async XLA Ops:
  7.2 1.2 copy-start.2
  7.2 211.9 %all-gather.7.cloned.1.call-start = ((), (), s32[]{:S(2)}) async-start(), calls=%async_computation.7 | async-start | bytes 11796480 | tf_op jit(solution)/shard_map/all_gather | solution.py:71
  14.4 55.7 %all-to-all-start = ((bf16[4,2,55296]{2,1,0:T(2,128)(2,1)}), bf16[4,2,55296]{2,1,0:T(2,128)(2,1)S(1)}, u32[]{:S(2)}, u32[]{:S(2)}) async-start(bf16[4,2,55296]{2,1,0:T(2,128)(2,1)} %reshape.134), calls=%async_computation | async-start | bytes 1769472 | tf_op jit(solution)/shard_map/all_to_all | solution.py:59
  74.8 0.8 copy-start.55
  74.8 0.8 copy-start.56
  74.8 0.8 copy-start.57
  74.8 0.8 copy-start.58
  74.8 0.8 copy-start.59
  74.8 0.8 copy-start.60
  74.8 0.8 copy-start.61
  74.8 0.8 copy-start.62
  74.8 0.8 copy-start.63
  74.8 0.8 copy-start.64
  74.9 0.8 copy-start.65
  74.9 0.8 copy-start.66
  74.9 0.8 copy-start.67
  74.9 0.8 copy-start.68
  74.9 0.8 copy-start.69
  74.9 0.8 copy-start.70
  74.9 0.8 copy-start.71
  74.9 0.8 copy-start.72
  74.9 0.8 copy-start.73
  74.9 0.8 copy-start.74
  75.0 0.8 copy-start.75
  75.0 0.8 copy-start.76
  75.0 0.8 copy-start.77
  75.0 0.8 copy-start.78
  75.0 0.8 copy-start.79
  96.2 59.7 %all-to-all-start.1 = ((bf16[96,48,96]{2,1,0:T(8,128)(2,1)}), bf16[96,48,96]{2,1,0:T(8,128)(2,1)S(1)}, u32[]{:S(2)}, u32[]{:S(2)}) async-start(bf16[96,48,96]{2,1,0:T(8,128)(2,1)} %fusion.115), calls=%async_computation.1 | async-start | bytes 2359296 | tf_op jit(solution)/shard_map/all_to_all | solution.py:66
  99.7 171.1 %all-gather.5.cloned.1.call-start = ((), (), s32[]{:S(2)}) async-start(), calls=%async_computation.6 | async-start | bytes 7962624 | tf_op jit(solution)/shard_map/all_gather | solution.py:87
  100.5 79.1 %copy-start.11 = (f32[384]{0:T(512)}, f32[384]{0:T(512)S(1)}, u32[]{:S(2)}) copy-start(f32[384]{0:T(512)S(1)} %dynamic_slice.13) | copy-start | bytes 4612
  157.5 24.7 %copy-start = (bf16[24,48,384]{2,1,0:T(8,128)(2,1)}, bf16[24,48,384]{2,1,0:T(8,128)(2,1)S(1)}, u32[]{:S(2)}) copy-start(bf16[24,48,384]{2,1,0:T(8,128)(2,1)S(1)} %all_to_all.59) | copy-start | bytes 2654212
  180.2 90.6 %copy-start.95 = (f32[1536]{0:T(1024)S(1)}, f32[1536]{0:T(1024)}, u32[]{:S(2)}) copy-start(f32[1536]{0:T(1024)} %param.16) | copy-start | bytes 18436
  181.5 257.6 %all-gather.9.cloned.1.call-start = ((), (), s32[]{:S(2)}) async-start(), calls=%async_computation.8 | async-start | bytes 11796480 | tf_op jit(solution)/shard_map/all_gather | solution.py:72
  182.3 361.6 %reduce-scatter.7.cloned.1.call-start = ((), (), s32[]{:S(2)}) async-start(), calls=%async_computation.10 | async-start | bytes 7962624
  480.1 65.5 %copy-start.14 = (f32[384]{0:T(512)S(1)}, f32[384]{0:T(512)}, u32[]{:S(2)}) copy-start(f32[384]{0:T(512)} %param.18) | copy-start | bytes 4612
  480.1 65.7 %copy-start.3 = (bf16[24,48,384]{2,1,0:T(8,128)(2,1)S(1)}, bf16[24,48,384]{2,1,0:T(8,128)(2,1)}, u32[]{:S(2)}) copy-start(bf16[24,48,384]{2,1,0:T(8,128)(2,1)} %param.10) | copy-start | bytes 2654212
  480.1 65.7 %copy-start.4 = (bf16[24,48,384]{2,1,0:T(8,128)(2,1)S(1)}, bf16[24,48,384]{2,1,0:T(8,128)(2,1)}, u32[]{:S(2)}) copy-start(bf16[24,48,384]{2,1,0:T(8,128)(2,1)} %param.11) | copy-start | bytes 2654212
  480.1 65.7 %copy-start.13 = (f32[384]{0:T(512)S(1)}, f32[384]{0:T(512)}, u32[]{:S(2)}) copy-start(f32[384]{0:T(512)} %param.19) | copy-start | bytes 4612
  480.1 117.7 %all-gather.11.cloned.1.call-start = ((), (), s32[]{:S(2)}) async-start(), calls=%async_computation.9 | async-start | bytes 7962624 | tf_op jit(solution)/shard_map/all_gather | solution.py:109
  547.5 160.6 %reduce-scatter.9.cloned.1.call-start = ((), (), s32[]{:S(2)}) async-start(), calls=%async_computation.11 | async-start | bytes 7962624
  642.5 67.4 %copy-start.12 = (f32[384]{0:T(512)S(1)}, f32[384]{0:T(512)}, u32[]{:S(2)}) copy-start(f32[384]{0:T(512)} %copy-done.11) | copy-start | bytes 4612
  642.5 67.6 %copy-start.1 = (bf16[24,48,384]{2,1,0:T(8,128)(2,1)S(1)}, bf16[24,48,384]{2,1,0:T(8,128)(2,1)}, u32[]{:S(2)}) copy-start(bf16[24,48,384]{2,1,0:T(8,128)(2,1)} %copy-done) | copy-start | bytes 2654212
  642.5 67.6 %copy-start.8 = (f32[1152]{0:T(1024)S(1)}, f32[1152]{0:T(1024)}, u32[]{:S(2)}) copy-start(f32[1152]{0:T(1024)} %copy-done.7) | copy-start | bytes 13828
  642.5 67.6 %copy-start.10 = (f32[1152]{0:T(1024)S(1)}, f32[1152]{0:T(1024)}, u32[]{:S(2)}) copy-start(f32[1152]{0:T(1024)} %copy-done.9) | copy-start | bytes 13828
  734.4 9.2 %copy-start.6 = (f32[7,7,384]{2,1,0:T(8,128)S(1)}, f32[7,7,384]{2,1,0:T(8,128)}, u32[]{:S(2)}) copy-start(f32[7,7,384]{2,1,0:T(8,128)} %param.12) | copy-start | bytes 225796
  739.1 27.7 %all-to-all-start.2 = ((bf16[4,2,55296]{2,1,0:T(2,128)(2,1)}), bf16[4,2,55296]{2,1,0:T(2,128)(2,1)S(1)}, u32[]{:S(2)}, u32[]{:S(2)}) async-start(bf16[4,2,55296]{2,1,0:T(2,128)(2,1)} %reshape.136), calls=%async_computation.2 | async-start | bytes 1769472 | tf_op jit(solution)/shard_map/all_to_all | solution.py:59
  823.1 1.7 copy-start.5
  (57 other events, 45.3 us)
Sparse Core Ops, SparseCore 0:
  9.6 209.4 all-gather.6
  221.5 49.2 all-gather.4
  272.4 166.7 all-gather.8
  480.2 63.5 reduce-scatter.6
  547.6 50.2 all-gather.10
  642.6 65.4 reduce-scatter.8
where the time goes:
time: 841 us; the launch traced here: 833 us
  waiting for transfers between devices  544 us (65%)
  matrix products  82.3 us (10%)
  blocking collectives  73.6 us (9%)
  local copies, waits for them, and re-layouts  54.9 us (7%)
  other arithmetic  48.8 us (6%)
  between operations  16 us (2%)
  starting transfers between devices  13.9 us (2%)
    all_gather x1, waiting for transfers between devices, body(): lax.all_gather(w_reduce, 'row', axis=1, tiled=True)  151 us
    unnamed x8, waiting for transfers between devices  131 us
    all_to_all x2, waiting for transfers between devices, mixing(): lax.all_to_all(source_field, 'row', split_axis=2, concat_axis=0, tiled=True)  68.8 us
    all_to_all x1, waiting for transfers between devices, mixing(): lax.all_to_all(mixed_out, 'row', split_axis=0, concat_axis=2, tiled=True)  54.6 us
    all_gather x1, waiting for transfers between devices, body(): lax.all_gather(normed, 'col', axis=1, tiled=True)  51.8 us
    all_gather x1, waiting for transfers between devices, body(): lax.all_gather(grad_branch, 'col', axis=1, tiled=True)  50.2 us
    psum x2, blocking collectives, channel_sums(): return lax.psum((first_sum, second_sum), 'col')  42.6 us
    unnamed x201, local copies, waits for them, and re-layouts  40.5 us
  transfers between devices with their start and end apart: 9, of which 9 were waited for; matrix products, arithmetic and copies ran while one was open for 7% of the time, Pallas kernels for 0%

commit v1 on v0

--- a/solution.py
+++ b/solution.py
@@ -7,6 +7,22 @@
 epsilon = 1e-06
 root_half = 0.7071067811865476
 density_scale = 0.3989422804014327
+
+
+def collect(x, axis, dim):
+    ways, here, hop = (lax.axis_size(axis), lax.axis_index(axis), x.shape[dim])
+    shape = [n * ways if d == dim else n for d, n in enumerate(x.shape)]
+    full = lax.dynamic_update_slice_in_dim(jnp.zeros(shape, x.dtype), x, here * hop, axis=dim)
+    going_up = going_down = x
+    for far in range(1, ways // 2 + 1):
+        going_up = lax.ppermute(going_up, axis, [(d, (d + 1) % ways) for d in range(ways)])
+        full = lax.dynamic_update_slice_in_dim(full, going_up, (here - far) % ways * hop, axis=dim)
+        if 2 * far < ways:
+            going_down = lax.ppermute(going_down, axis, [(d, (d - 1) % ways) for d in range(ways)])
+            full = lax.dynamic_update_slice_in_dim(
+                full, going_down, (here + far) % ways * hop, axis=dim
+            )
+    return full
 
 
 def spatial_mix(padded, weights, height):
@@ -106,7 +122,7 @@
     grad_branch = (layer_scale * cot_f).reshape(tokens, narrow).astype(jnp.bfloat16)
     panel = reduce_full
     grad_hidden = lax.dot_general(
-        lax.all_gather(grad_branch, "col", axis=1, tiled=True),
+        collect(grad_branch, "col", 1),
         panel,
         (((1,), (1,)), ((), ())),
         preferred_element_type=jnp.float32,

time: 841 us -> 868 us (1.032)
  starting transfers between devices: 13.9 us -> 36.6 us
    all_gather x1 -> x0, waiting for transfers between devices: 50.2 us -> none  [body(): lax.all_gather(grad_branch, 'col', axis=1, tiled=True)]
    ppermute x0 -> x7, waiting for transfers between devices: none -> 43 us  [the longest x4 42.3 us: collect(): lax.ppermute(going_up, axis, [(d, (d + 1) % ways) for d in range(ways)])]
    ppermute x0 -> x7, starting transfers between devices: none -> 22.9 us  [the longest x4 19.1 us: collect(): lax.ppermute(going_up, axis, [(d, (d + 1) % ways) for d in range(ways)])]
    unnamed x8 -> x7, waiting for transfers between devices: 131 us -> 141 us
    unnamed x201 -> x205, local copies, waits for them, and re-layouts: 40.5 us -> 41 us
  transfers between devices with their start and end apart: 9 -> 15, of which waited for: 9 -> 13; matrix products, arithmetic and copies ran while one was open for 7% -> 7% of each run, Pallas kernels for 0% -> 0%
where the time goes in v1:
time: 868 us; the launch traced here: 861 us
  waiting for transfers between devices  546 us (63%)
  matrix products  80.2 us (9%)
  blocking collectives  73.6 us (8%)
  local copies, waits for them, and re-layouts  59.5 us (7%)
  other arithmetic  48.5 us (6%)
  starting transfers between devices  36.6 us (4%)
  between operations  15.7 us (2%)
    all_gather x1, waiting for transfers between devices, body(): lax.all_gather(w_reduce, 'row', axis=1, tiled=True)  151 us
    unnamed x7, waiting for transfers between devices  141 us
    all_to_all x2, waiting for transfers between devices, mixing(): lax.all_to_all(source_field, 'row', split_axis=2, concat_axis=0, tiled=True)  68.8 us
    all_to_all x1, waiting for transfers between devices, mixing(): lax.all_to_all(mixed_out, 'row', split_axis=0, concat_axis=2, tiled=True)  54.6 us
    all_gather x1, waiting for transfers between devices, body(): lax.all_gather(normed, 'col', axis=1, tiled=True)  51.8 us
    psum x2, blocking collectives, channel_sums(): return lax.psum((first_sum, second_sum), 'col')  42.6 us
    ppermute x4, waiting for transfers between devices, collect(): lax.ppermute(going_up, axis, [(d, (d + 1) % ways) for d in range(ways)])  42.3 us
    unnamed x205, local copies, waits for them, and re-layouts  41 us
  transfers between devices with their start and end apart: 15, of which 13 were waited for; matrix products, arithmetic and copies ran while one was open for 7% of the time, Pallas kernels for 0%

profile of v1, /device:TPU:2, one launch (start us, length us, event | category | flops | bytes accessed | tf_op | source)
XLA Modules:
  0.0 860.5 jit_solution(9503604934700878326)
XLA Ops:
  8.3 1.4 copy.16
  9.8 4.6 reshape.134
  14.4 4.9 all-to-all-start
  21.0 2.2 fusion.181
  23.2 46.8 %all-to-all-done = bf16[4,2,55296]{2,1,0:T(2,128)(2,1)S(1)} async-done(((bf16[4,2,55296]{2,1,0:T(2,128)(2,1)}), bf16[4,2,55296]{2,1,0:T(2,128)(2,1)S(1)}, u32[]{:S(2)}, u32[]{:S(2)}) %all-to-all-start) | async-done | bytes 884768 | tf_op jit(solution)/shard_map/all_to_all | solution.py:75
  70.1 2.4 reshape.135
  72.5 2.1 copy.24
  76.0 20.1 %fusion.115 = bf16[96,48,96]{2,1,0:T(8,128)(2,1)} fusion(f32[102,54,96]{2,1,0:T(8,128)S(1)} %pad_convert_fusion.1, f32[96]{0:T(128)} %get-tuple-element.105, f32[96]{0:T(128)S(1)} %get-tuple-element.58, f32[96]{0:T(128)S(1)} %get-tuple-element.59, f32[96]{0:T(128)S(1)} %get-tuple-element.60, f32[96]{0:T(128)S(1)} %copy-done.57, f32[96]{0:T(128)S(1)} %copy-done.58, ...), kind=kLoop, calls=%fused_computation.178 | loop fusion | flops 46006272 | bytes 87608256 | tf_op jit(solution)/shard_map/convert_element_type | solution.py:81
  96.1 3.5 all-to-all-start.1
  101.2 54.6 %all-to-all-done.1 = bf16[96,48,96]{2,1,0:T(8,128)(2,1)S(1)} async-done(((bf16[96,48,96]{2,1,0:T(8,128)(2,1)}), bf16[96,48,96]{2,1,0:T(8,128)(2,1)S(1)}, u32[]{:S(2)}, u32[]{:S(2)}) %all-to-all-start.1) | async-done | bytes 884768 | tf_op jit(solution)/shard_map/all_to_all | solution.py:82
  155.9 0.9 copy.19
  158.1 21.4 %all-reduce.3 = (f32[1152]{0:T(1024)S(1)}, f32[1152]{0:T(1024)S(1)}) all-reduce(f32[1152]{0:T(1024)S(1)} %reduce_sum.43, f32[1152]{0:T(1024)S(1)} %reduce_sum.41), channel_id=1, replica_groups=mesh['row'=4,'col'=8] {'col'}, use_global_device_ids=true, to_apply=%region_3.4 | all-reduce | flops 2304 | bytes 18432 | tf_op jit(solution)/shard_map/psum | solution.py:53
  180.2 1.3 add_convert_fusion.1
  182.8 36.2 %all-gather.6.cloned.1.call-done = bf16[3072,1536]{1,0:T(8,128)(2,1)} async-done(((bf16[768,1536]{1,0:T(8,128)(2,1)}), bf16[3072,1536]{1,0:T(8,128)(2,1)}) %all-gather.6.cloned.1.call-update) | async-done | bytes 9437200 | tf_op jit(solution)/shard_map/all_gather | solution.py:87
  219.0 51.8 %all-gather.4.cloned.1.call-done = bf16[1152,3072]{1,0:T(8,128)(2,1)} async-done(((bf16[1152,384]{1,0:T(8,128)(2,1)}), bf16[1152,3072]{1,0:T(8,128)(2,1)}) %all-gather.4.cloned.1.call-update) | async-done | bytes 7077904 | tf_op jit(solution)/shard_map/all_gather | solution.py:103
  270.8 17.0 %convolution_add_fusion = f32[1152,1536]{1,0:T(8,128)} fusion(bf16[1152,3072]{1,0:T(8,128)(2,1)} %all-gather.4.cloned.1.call-done, bf16[3072,1536]{1,0:T(8,128)(2,1)} %all-gather.6.cloned.1.call-done, f32[1536]{0:T(1024)S(1)} %copy-done.97), kind=kOutput, calls=%fused_computation.7 | convolution fusion | flops 10873405440 | bytes 23599104 | tf_op jit(solution)/shard_map/dot_general | solution.py:102
  287.8 151.4 %all-gather.8.cloned.1.call-done = bf16[1536,3072]{1,0:T(8,128)(2,1)} async-done(((bf16[1536,768]{1,0:T(8,128)(2,1)}), bf16[1536,3072]{1,0:T(8,128)(2,1)}) %all-gather.8.cloned.1.call-update) | async-done | bytes 9437200 | tf_op jit(solution)/shard_map/all_gather | solution.py:88
  439.2 31.1 %fusion = bf16[3072,1152]{0,1:T(8,128)(2,1)} fusion(bf16[1536,3072]{1,0:T(8,128)(2,1)} %all-gather.8.cloned.1.call-done, f32[1152,1536]{1,0:T(8,128)} %convolution_add_fusion), kind=kOutput, calls=%fused_computation.5 | convolution fusion | flops 10990190592 | bytes 23592960 | tf_op jit(solution)/shard_map/dot_general | solution.py:109
  470.2 9.6 %copy.26 = bf16[3072,1152]{1,0:T(8,128)(2,1)} copy(bf16[3072,1152]{0,1:T(8,128)(2,1)} %fusion) | data formatting | bytes 14155776
  480.0 63.7 %reduce-scatter.7.cloned.1.call-done = bf16[384,1152]{1,0:T(8,128)(2,1)} async-done(((bf16[3072,1152]{1,0:T(8,128)(2,1)}), bf16[384,1152]{1,0:T(8,128)(2,1)}) %reduce-scatter.7.cloned.1.call-update) | async-done | bytes 884752
  543.7 1.7 copy.27
  545.6 1.4 fusion.167
  547.0 1.7 collective-permute-start.1
  548.7 18.3 %collective-permute-done = bf16[1152,384]{1,0:T(8,128)(2,1)S(1)} collective-permute-done((bf16[1152,384]{1,0:T(8,128)(2,1)S(1)}, bf16[1152,384]{1,0:T(8,128)(2,1)S(1)}, u32[]{:S(2)}, u32[]{:S(2)}) %collective-permute-start) | collective-permute-done | bytes 884768 | tf_op jit(solution)/shard_map/ppermute | solution.py:18
  567.9 2.0 collective-permute-start.3
  569.9 15.0 %collective-permute-done.2 = bf16[1152,384]{1,0:T(8,128)(2,1)S(1)} collective-permute-done((bf16[1152,384]{1,0:T(8,128)(2,1)S(1)}, bf16[1152,384]{1,0:T(8,128)(2,1)S(1)}, u32[]{:S(2)}, u32[]{:S(2)}) %collective-permute-start.2) | collective-permute-done | bytes 884768 | tf_op jit(solution)/shard_map/ppermute | solution.py:18
  584.9 4.9 collective-permute-start.4
  592.2 1.4 constant_dynamic-update-slice_fusion.5
  593.6 4.9 collective-permute-done.4
  598.5 14.0 %collective-permute-start.6 = (bf16[1152,384]{1,0:T(8,128)(2,1)S(1)}, bf16[1152,384]{1,0:T(8,128)(2,1)S(1)}, u32[]{:S(2)}, u32[]{:S(2)}) collective-permute-start(bf16[1152,384]{1,0:T(8,128)(2,1)S(1)} %collective-permute-done.4), channel_id=1, source_target_pairs={{0,1},{1,2},{2,3},{3,4},{4,5},{5,6},{6,7},{7,0},{8,9},{9,10},{10,1... | collective-permute-start | bytes 2654216 | tf_op jit(solution)/shard_map/ppermute | solution.py:18
  613.5 4.1 collective-permute-done.6
  617.9 16.6 %fusion.2.clone.4 = bf16[1152,1536]{1,0:T(8,128)(2,1)S(1)} fusion(bf16[1152,3072]{1,0:T(8,128)(2,1)S(1)} %constant_dynamic-update-slice_fusion, bf16[1536,3072]{1,0:T(8,128)(2,1)} %all-gather.8.cloned.1.call-done, f32[1152,1536]{1,0:T(8,128)} %convolution_add_fusion), kind=kOutput, calls=%fused_computation.8.clone.clone.clone.1 | convolution fusion | flops 10889330688 | bytes 27131904 | tf_op jit(solution)/shard_map/dot_general | solution.py:124
  634.5 15.6 %fusion.1 = bf16[3072,1152]{0,1:T(8,128)(2,1)} fusion(bf16[3072,1536]{1,0:T(8,128)(2,1)} %all-gather.6.cloned.1.call-done, bf16[1152,1536]{1,0:T(8,128)(2,1)S(1)} %fusion.2.clone.4), kind=kOutput, calls=%fused_computation.6 | convolution fusion | flops 10875174912 | bytes 20054016 | tf_op jit(solution)/shard_map/dot_general | solution.py:133
  650.1 10.1 %copy.28 = bf16[3072,1152]{1,0:T(8,128)(2,1)} copy(bf16[3072,1152]{0,1:T(8,128)(2,1)} %fusion.1) | data formatting | bytes 14155776
  660.3 75.5 %reduce-scatter.9.cloned.1.call-done = bf16[384,1152]{1,0:T(8,128)(2,1)} async-done(((bf16[3072,1152]{1,0:T(8,128)(2,1)}), bf16[384,1152]{1,0:T(8,128)(2,1)}) %reduce-scatter.9.cloned.1.call-update) | async-done | bytes 884752
  735.9 1.7 copy.29
  738.7 21.2 %all-reduce.2 = (f32[1152]{0:T(1024)S(1)}, f32[1152]{0:T(1024)S(1)}) all-reduce(f32[1152]{0:T(1024)S(1)} %fusion.172, f32[1152]{0:T(1024)S(1)} %fusion.174), channel_id=1, replica_groups=mesh['row'=4,'col'=8] {'col'}, use_global_device_ids=true, to_apply=%region_9.10 | all-reduce | flops 2304 | bytes 18432 | tf_op jit(solution)/shard_map/psum | solution.py:53
  759.8 1.0 fusion.171
  760.8 1.4 copy.20
  762.3 4.6 reshape.136
  766.9 4.6 all-to-all-start.2
  771.6 1.0 fusion.180
  772.6 22.0 %all-to-all-done.2 = bf16[4,2,55296]{2,1,0:T(2,128)(2,1)S(1)} async-done(((bf16[4,2,55296]{2,1,0:T(2,128)(2,1)}), bf16[4,2,55296]{2,1,0:T(2,128)(2,1)S(1)}, u32[]{:S(2)}, u32[]{:S(2)}) %all-to-all-start.2) | async-done | bytes 884768 | tf_op jit(solution)/shard_map/all_to_all | solution.py:75
  794.6 2.4 reshape.137
  797.0 2.1 copy.25
  800.5 19.4 %fusion.60 = bf16[96,48,96]{2,1,0:T(8,128)(2,1)S(1)} fusion(f32[102,54,96]{2,1,0:T(8,128)S(1)} %pad_convert_fusion, f32[96]{0:T(128)} %get-tuple-element.56, f32[96]{0:T(128)S(1)} %get-tuple-element.9, f32[96]{0:T(128)S(1)} %get-tuple-element.10, f32[96]{0:T(128)S(1)} %get-tuple-element.11, f32[96]{0:T(128)S(1)} %copy-done.17, f32[96]{0:T(128)S(1)} %copy-done.18, ...), kind=kLoop, calls=%fused_computation.74 | loop fusion | flops 46006272 | bytes 87608256 | tf_op jit(solution)/shard_map/convert_element_type | solution.py:81
  819.9 31.0 %all_to_all.72 = bf16[96,48,96]{2,1,0:T(8,128)(2,1)S(1)} all-to-all(bf16[96,48,96]{2,1,0:T(8,128)(2,1)S(1)} %fusion.60), channel_id=1, replica_groups=mesh['row'=4,'col'=8] {'row'}, dimensions={0} | all-to-all | bytes 1769472 | tf_op jit(solution)/shard_map/all_to_all | solution.py:82
  852.6 1.1 fusion.168
  (241 shorter events, 16.6 us)
Async XLA Ops:
  7.2 1.2 copy-start.2
  7.2 211.9 %all-gather.6.cloned.1.call-start = ((), (), s32[]{:S(2)}) async-start(), calls=%async_computation.7 | async-start | bytes 11796480 | tf_op jit(solution)/shard_map/all_gather | solution.py:87
  14.4 55.7 %all-to-all-start = ((bf16[4,2,55296]{2,1,0:T(2,128)(2,1)}), bf16[4,2,55296]{2,1,0:T(2,128)(2,1)S(1)}, u32[]{:S(2)}, u32[]{:S(2)}) async-start(bf16[4,2,55296]{2,1,0:T(2,128)(2,1)} %reshape.134), calls=%async_computation | async-start | bytes 1769472 | tf_op jit(solution)/shard_map/all_to_all | solution.py:75
  74.8 0.8 copy-start.57
  74.8 0.8 copy-start.58
  74.8 0.8 copy-start.59
  74.8 0.8 copy-start.60
  74.8 0.8 copy-start.61
  74.8 0.8 copy-start.62
  74.8 0.8 copy-start.63
  74.8 0.8 copy-start.64
  74.8 0.8 copy-start.65
  74.8 0.8 copy-start.66
  74.9 0.8 copy-start.67
  74.9 0.8 copy-start.68
  74.9 0.8 copy-start.69
  74.9 0.8 copy-start.70
  74.9 0.8 copy-start.71
  74.9 0.8 copy-start.72
  74.9 0.8 copy-start.73
  96.1 59.8 %all-to-all-start.1 = ((bf16[96,48,96]{2,1,0:T(8,128)(2,1)}), bf16[96,48,96]{2,1,0:T(8,128)(2,1)S(1)}, u32[]{:S(2)}, u32[]{:S(2)}) async-start(bf16[96,48,96]{2,1,0:T(8,128)(2,1)} %fusion.115), calls=%async_computation.1 | async-start | bytes 2359296 | tf_op jit(solution)/shard_map/all_to_all | solution.py:82
  99.6 171.2 %all-gather.4.cloned.1.call-start = ((), (), s32[]{:S(2)}) async-start(), calls=%async_computation.6 | async-start | bytes 7962624 | tf_op jit(solution)/shard_map/all_gather | solution.py:103
  101.2 78.4 %copy-start.13 = (f32[384]{0:T(512)}, f32[384]{0:T(512)S(1)}, u32[]{:S(2)}) copy-start(f32[384]{0:T(512)S(1)} %dynamic_slice.13) | copy-start | bytes 4612
  157.5 24.7 %copy-start = (bf16[24,48,384]{2,1,0:T(8,128)(2,1)}, bf16[24,48,384]{2,1,0:T(8,128)(2,1)S(1)}, u32[]{:S(2)}) copy-start(bf16[24,48,384]{2,1,0:T(8,128)(2,1)S(1)} %all_to_all.59) | copy-start | bytes 2654212
  180.2 90.6 %copy-start.97 = (f32[1536]{0:T(1024)S(1)}, f32[1536]{0:T(1024)}, u32[]{:S(2)}) copy-start(f32[1536]{0:T(1024)} %param.16) | copy-start | bytes 18436
  181.5 257.6 %all-gather.8.cloned.1.call-start = ((), (), s32[]{:S(2)}) async-start(), calls=%async_computation.8 | async-start | bytes 11796480 | tf_op jit(solution)/shard_map/all_gather | solution.py:88
  182.3 361.4 %reduce-scatter.7.cloned.1.call-start = ((), (), s32[]{:S(2)}) async-start(), calls=%async_computation.9 | async-start | bytes 7962624
  479.9 65.5 %copy-start.16 = (f32[384]{0:T(512)S(1)}, f32[384]{0:T(512)}, u32[]{:S(2)}) copy-start(f32[384]{0:T(512)} %param.18) | copy-start | bytes 4612
  479.9 65.7 %copy-start.3 = (bf16[24,48,384]{2,1,0:T(8,128)(2,1)S(1)}, bf16[24,48,384]{2,1,0:T(8,128)(2,1)}, u32[]{:S(2)}) copy-start(bf16[24,48,384]{2,1,0:T(8,128)(2,1)} %param.10) | copy-start | bytes 2654212
  479.9 65.7 %copy-start.4 = (bf16[24,48,384]{2,1,0:T(8,128)(2,1)S(1)}, bf16[24,48,384]{2,1,0:T(8,128)(2,1)}, u32[]{:S(2)}) copy-start(bf16[24,48,384]{2,1,0:T(8,128)(2,1)} %param.11) | copy-start | bytes 2654212
  479.9 65.7 %copy-start.15 = (f32[384]{0:T(512)S(1)}, f32[384]{0:T(512)}, u32[]{:S(2)}) copy-start(f32[384]{0:T(512)} %param.19) | copy-start | bytes 4612
  479.9 255.9 %reduce-scatter.9.cloned.1.call-start = ((), (), s32[]{:S(2)}) async-start(), calls=%async_computation.10 | async-start | bytes 7962624
  547.0 20.0 %collective-permute-start = (bf16[1152,384]{1,0:T(8,128)(2,1)S(1)}, bf16[1152,384]{1,0:T(8,128)(2,1)S(1)}, u32[]{:S(2)}, u32[]{:S(2)}) collective-permute-start(bf16[1152,384]{1,0:T(8,128)(2,1)S(1)} %bitcast.271), channel_id=1, source_target_pairs={{0,1},{1,2},{2,3},{3,4},{4,5},{5,6},{6,7},{7,0},{8,9},{9,10},{10,1... | collective-permute-start | bytes 2654216 | tf_op jit(solution)/shard_map/ppermute | solution.py:18
  547.0 20.9 %collective-permute-start.1 = (bf16[1152,384]{1,0:T(8,128)(2,1)S(1)}, bf16[1152,384]{1,0:T(8,128)(2,1)}, u32[]{:S(2)}, u32[]{:S(2)}) collective-permute-start(bf16[1152,384]{1,0:T(8,128)(2,1)S(1)} %bitcast.272), channel_id=1, source_target_pairs={{0,7},{1,0},{2,1},{3,2},{4,3},{5,4},{6,5},{7,6},{8,15},{9,8},{10,9... | collective-permute-start | bytes 2654216 | tf_op jit(solution)/shard_map/ppermute | solution.py:21
  567.0 17.9 %copy-start.6 = (bf16[1152,384]{1,0:T(8,128)(2,1)}, bf16[1152,384]{1,0:T(8,128)(2,1)S(1)}, u32[]{:S(2)}) copy-start(bf16[1152,384]{1,0:T(8,128)(2,1)S(1)} %collective-permute-done) | copy-start | bytes 2654212
  567.0 17.9 %collective-permute-start.2 = (bf16[1152,384]{1,0:T(8,128)(2,1)S(1)}, bf16[1152,384]{1,0:T(8,128)(2,1)S(1)}, u32[]{:S(2)}, u32[]{:S(2)}) collective-permute-start(bf16[1152,384]{1,0:T(8,128)(2,1)S(1)} %collective-permute-done), channel_id=1, source_target_pairs={{0,1},{1,2},{2,3},{3,4},{4,5},{5,6},{6,7},{7,0},{8,9},{9,10},{10,1... | collective-permute-start | bytes 2654216 | tf_op jit(solution)/shard_map/ppermute | solution.py:18
  567.9 24.2 %collective-permute-start.3 = (bf16[1152,384]{1,0:T(8,128)(2,1)}, bf16[1152,384]{1,0:T(8,128)(2,1)S(1)}, u32[]{:S(2)}, u32[]{:S(2)}) collective-permute-start(bf16[1152,384]{1,0:T(8,128)(2,1)} %collective-permute-done.1), channel_id=1, source_target_pairs={{0,7},{1,0},{2,1},{3,2},{4,3},{5,4},{6,5},{7,6},{8,15},{9,8},{10,9... | collective-permute-start | bytes 2654216 | tf_op jit(solution)/shard_map/ppermute | solution.py:21
  584.9 13.6 %collective-permute-start.4 = (bf16[1152,384]{1,0:T(8,128)(2,1)S(1)}, bf16[1152,384]{1,0:T(8,128)(2,1)S(1)}, u32[]{:S(2)}, u32[]{:S(2)}) collective-permute-start(bf16[1152,384]{1,0:T(8,128)(2,1)S(1)} %collective-permute-done.2), channel_id=1, source_target_pairs={{0,1},{1,2},{2,3},{3,4},{4,5},{5,6},{6,7},{7,0},{8,9},{9,10},{10,1... | collective-permute-start | bytes 2654216 | tf_op jit(solution)/shard_map/ppermute | solution.py:18
  590.7 1.2 copy-start.7
  592.1 21.1 %collective-permute-start.5 = (bf16[1152,384]{1,0:T(8,128)(2,1)S(1)}, bf16[1152,384]{1,0:T(8,128)(2,1)S(1)}, u32[]{:S(2)}, u32[]{:S(2)}) collective-permute-start(bf16[1152,384]{1,0:T(8,128)(2,1)S(1)} %collective-permute-done.3), channel_id=1, source_target_pairs={{0,7},{1,0},{2,1},{3,2},{4,3},{5,4},{6,5},{7,6},{8,15},{9,8},{10,9... | collective-permute-start | bytes 2654216 | tf_op jit(solution)/shard_map/ppermute | solution.py:21
  598.5 19.2 %collective-permute-start.6 = (bf16[1152,384]{1,0:T(8,128)(2,1)S(1)}, bf16[1152,384]{1,0:T(8,128)(2,1)S(1)}, u32[]{:S(2)}, u32[]{:S(2)}) collective-permute-start(bf16[1152,384]{1,0:T(8,128)(2,1)S(1)} %collective-permute-done.4), channel_id=1, source_target_pairs={{0,1},{1,2},{2,3},{3,4},{4,5},{5,6},{6,7},{7,0},{8,9},{9,10},{10,1... | collective-permute-start | bytes 2654216 | tf_op jit(solution)/shard_map/ppermute | solution.py:18
  660.3 77.3 %copy-start.10 = (f32[1152]{0:T(1024)S(1)}, f32[1152]{0:T(1024)}, u32[]{:S(2)}) copy-start(f32[1152]{0:T(1024)} %copy-done.9) | copy-start | bytes 13828
  660.3 77.4 %copy-start.12 = (f32[1152]{0:T(1024)S(1)}, f32[1152]{0:T(1024)}, u32[]{:S(2)}) copy-start(f32[1152]{0:T(1024)} %copy-done.11) | copy-start | bytes 13828
  660.3 77.4 %copy-start.14 = (f32[384]{0:T(512)S(1)}, f32[384]{0:T(512)}, u32[]{:S(2)}) copy-start(f32[384]{0:T(512)} %copy-done.13) | copy-start | bytes 4612
  660.3 77.3 %copy-start.1 = (bf16[24,48,384]{2,1,0:T(8,128)(2,1)S(1)}, bf16[24,48,384]{2,1,0:T(8,128)(2,1)}, u32[]{:S(2)}) copy-start(bf16[24,48,384]{2,1,0:T(8,128)(2,1)} %copy-done) | copy-start | bytes 2654212
  762.2 9.2 %copy-start.8 = (f32[7,7,384]{2,1,0:T(8,128)S(1)}, f32[7,7,384]{2,1,0:T(8,128)}, u32[]{:S(2)}) copy-start(f32[7,7,384]{2,1,0:T(8,128)} %param.12) | copy-start | bytes 225796
  766.9 27.7 %all-to-all-start.2 = ((bf16[4,2,55296]{2,1,0:T(2,128)(2,1)}), bf16[4,2,55296]{2,1,0:T(2,128)(2,1)S(1)}, u32[]{:S(2)}, u32[]{:S(2)}) async-start(bf16[4,2,55296]{2,1,0:T(2,128)(2,1)} %reshape.136), calls=%async_computation.2 | async-start | bytes 1769472 | tf_op jit(solution)/shard_map/all_to_all | solution.py:75
  850.9 1.7 copy-start.5
  (65 other events, 51.7 us)
Sparse Core Ops, SparseCore 0:
  9.6 209.4 all-gather.5
  221.5 49.2 all-gather.3
  272.4 166.7 all-gather.7
  480.0 63.5 reduce-scatter.6
  660.4 75.3 reduce-scatter.8
